TPU v7x, 32 devices: a whole 2x2x4 slice. The times are simulated.
32 devices in a mesh: tm: 4 (over y, x), space: 8 (over z, core).
Axes of the slice: x: 2, y: 2, z: 4, core: 2. Of those that a mesh axis runs over, the one named last changes fastest.
Arguments:
- initial: float32 [32, 128, 128], P('space'), may hold values from -6 to 6
- guess: float32 [4, 32, 128, 128], P('tm', 'space'), may hold values from -6 to 6
- velocity: float32 [4, 3, 32, 128, 128], P(None, None, 'space'), may hold values from -0.6 to 0.6
- heat_shape: float32 [32, 128, 128], P('space'), may hold values from 0.002 to 0.02
- rack_map: int32 [32, 128], P('space'), may hold values from 0 to 63
- power: int32 [64, 64], P('tm'), may hold values from 0 to 7
- fan_mode: int32 [64], replicated, may hold values from 0 to 3
Outputs:
- states: float32 [64, 32, 128, 128], P('tm', 'space')
All inputs are finite; a program needn't handle non-finite values.
Results may differ from a plain program's by a relative error of at most 0.00029.
Values sent between devices are 32-bit elements; how exact they have to be, the bound alone decides.
A program may use at most 64 MiB of HBM per device.

v0:
```python
import jax
import jax.numpy as jnp
from jax import lax
from jax.sharding import PartitionSpec as P

SWEEPS = 2


DIFFUSE = 0.5


def padded_2(x, sides, width):
    for axis, dim in sides:
        peers, length = (lax.axis_size(axis), x.shape[dim])
        up = [(i, (i + 1) % peers) for i in range(peers - 1)]
        down = [(j, i) for i, j in up]
        last = lax.slice_in_dim(x, length - width, length, axis=dim)
        initial = lax.slice_in_dim(x, 0, width, axis=dim)
        before = lax.ppermute(last, axis, up)
        after = lax.ppermute(initial, axis, down)
        x = jnp.concatenate([before, x, after], axis=dim)
    return x


def passed_along(block, axis, distance):
    devices = range(lax.axis_size(axis))
    route = [(i - distance, i) for i in devices if i - distance in devices]
    return lax.ppermute(block, axis, route)


def jacobi_sweep(widened, source, courant, scale_ratio):
    diffusion = DIFFUSE * scale_ratio
    half_ratio = 0.5 * scale_ratio
    padded = jnp.pad(widened, ((0, 0), (1, 1), (1, 1)))
    summed = (
        source
        + (diffusion - half_ratio * courant[0]) * padded[2:, 1:-1, 1:-1]
        + (diffusion + half_ratio * courant[0]) * padded[:-2, 1:-1, 1:-1]
    )
    summed = (
        summed
        + (diffusion - half_ratio * courant[1]) * padded[1:-1, 2:, 1:-1]
        + (diffusion + half_ratio * courant[1]) * padded[1:-1, :-2, 1:-1]
    )
    summed = (
        summed
        + (diffusion - half_ratio * courant[2]) * padded[1:-1, 1:-1, 2:]
        + (diffusion + half_ratio * courant[2]) * padded[1:-1, 1:-1, :-2]
    )
    return summed / (1.0 + 6.0 * diffusion)


def local(initial, guess, velocity, heat_shape, rack_map, power, fan_mode):
    steps_dev = power.shape[0]
    rack_count = power.shape[1]
    block_index = lax.axis_index("tm")
    block_count = lax.axis_size("tm")
    onehot = (rack_map[:, :, None] == lax.iota(jnp.int32, rack_count)[None, None, :]).astype(
        jnp.float32
    )
    cell_power = jnp.einsum(
        "xyr,kr->kxy", onehot, power.astype(jnp.float32), precision=lax.Precision.HIGHEST
    )

    def implicit_solve(first_state, step_index, fan_index, scale_ratio):
        courant = lax.dynamic_index_in_dim(velocity, fan_index, 0, keepdims=False)
        if step_index is None:
            source = first_state
        else:
            power_now = lax.dynamic_index_in_dim(cell_power, step_index, 0, keepdims=False)
            source = first_state + heat_shape * power_now[:, :, None]
        current = first_state
        for sweep_index in range(SWEEPS):
            widened = padded_2(current, (("space", 0),), 1)
            current = jacobi_sweep(widened, source, courant, scale_ratio)
        return current

    def advance(current, step_index):
        fan_index = lax.dynamic_index_in_dim(
            fan_mode, block_index * steps_dev + step_index, 0, keepdims=False
        )
        return implicit_solve(current, step_index, fan_index, 1.0)

    previous_guess = passed_along(guess[0], "tm", 1)
    first_state = jnp.where(block_index == 0, initial, previous_guess)

    def first_pass(current, step_index):
        return (advance(current, step_index), None)

    final_state, unused = lax.scan(first_pass, first_state, jnp.arange(steps_dev))
    residual_own = final_state - guess[0]
    fan_index = lax.dynamic_index_in_dim(
        fan_mode, block_index * steps_dev + steps_dev - 1, 0, keepdims=False
    )
    correction = residual_own
    for section_index in range(block_count - 1):
        incoming = passed_along(correction, "tm", 1)
        correction = implicit_solve(incoming, None, fan_index, float(steps_dev)) + residual_own
    own_value = guess[0] + correction
    previous = passed_along(own_value, "tm", 1)
    second_state = jnp.where(block_index == 0, initial, previous)

    def second_pass(current, step_index):
        advanced = advance(current, step_index)
        return (advanced, advanced)

    unused_state, results = lax.scan(second_pass, second_state, jnp.arange(steps_dev - 1))
    return jnp.concatenate([results, own_value[None]], axis=0)


def solution(mesh):
    placed = (
        P("space", None, None),
        P("tm", "space", None, None),
        P(None, None, "space", None, None),
        P("space", None, None),
        P("space", None),
        P("tm", None),
        P(),
    )
    return jax.shard_map(
        local, mesh=mesh, in_specs=placed, out_specs=P("tm", "space", None, None), check_vma=False
    )
```

profile of v0, /device:TPU:15, one launch (start us, length us, event | category | flops | bytes accessed | tf_op | source)
XLA Modules:
  0.0 966.3 jit_solution(8049821929034357233)
XLA Ops:
  2.8 6.5 collective-permute-done.8
  10.0 421.5 %while.26 = (s32[]{:T(128)}, f32[4,128,128]{2,1,0:T(8,128)}, s32[16]{0:T(128)S(1)}, f32[16,4,128]{2,1,0:T(4,128)}, f32[4,128,128]{2,1,0:T(8,128)}, /*index=5*/s3...) while((s32[]{:T(128)}, f32[4,128,128]{2,1,0:T(8,128)}, ...), condition=%wide.region_1.2_spmd, body=%wide.region_0.1_spmd.sunk | while | flops 6449886 | bytes 9994951 | solution.py:90
  29.2 3.6 collective-permute-start.3
  55.5 3.6 collective-permute-start.3
  160.8 3.6 collective-permute-start.3
  434.1 7.2 collective-permute-done.9
  442.6 4.0 collective-permute-start.10
  457.9 3.6 collective-permute-start.13
  464.8 8.2 collective-permute-done.14
  473.0 3.7 collective-permute-start.15
  480.6 4.3 collective-permute-start.17
  490.2 7.2 collective-permute-done.19
  497.5 4.9 collective-permute-start.20
  506.3 4.3 collective-permute-start.22
  516.5 7.5 collective-permute-done.24
  525.7 435.9 %while.27 = (s32[]{:T(128)}, f32[4,128,128]{2,1,0:T(8,128)}, f32[15,4,128,128]{3,2,1,0:T(8,128)}, s32[15]{0:T(128)S(1)}, f32[16,4,128]{2,1,0:T(4,128)}, /*index=...) while((s32[]{:T(128)}, f32[4,128,128]{2,1,0:T(8,128)}, ...), condition=%wide.region_3.4_spmd, body=%wide.region_2.3_spmd.sunk | while | flops 6449886 | bytes 10257115 | solution.py:107
  527.2 4.9 collective-permute-start.4
  557.0 4.1 collective-permute-start.4
  586.0 4.1 collective-permute-start.4
  615.0 4.1 collective-permute-start.4
  644.0 4.1 collective-permute-start.4
  673.0 4.1 collective-permute-start.4
  702.0 4.1 collective-permute-start.4
  731.0 4.1 collective-permute-start.4
  760.1 4.1 collective-permute-start.4
  789.1 4.1 collective-permute-start.4
  818.1 4.1 collective-permute-start.4
  847.1 4.1 collective-permute-start.4
  876.1 4.1 collective-permute-start.4
  905.2 4.1 collective-permute-start.4
  934.1 4.1 collective-permute-start.4
  961.6 4.7 pad_maximum_fusion.8
  (637 shorter events, 689.5 us)
Async XLA Ops:
  10.9 13.2 %collective-permute-start = (f32[1,128,128]{2,1,0:T(8,128)S(1)}, f32[1,128,128]{2,1,0:T(8,128)S(1)}, u32[]{:S(2)}, u32[]{:S(2)}) collective-permute-start(f32[1,128,128]{2,1,0:T(8,128)S(1)} %get-tuple-element.403), channel_id=1, source_target_pairs={{1,0},{2,1},{3,2},{4,3},{5,4},{6,5},{7,6},{9,8},{10,9},{11,10},{12... | collective-permute-start | bytes 196616 | tf_op jit(solution)/shard_map/while/body/eval_jaxpr/ppermute | solution.py:20
  37.6 12.8 %collective-permute-start = (f32[1,128,128]{2,1,0:T(8,128)S(1)}, f32[1,128,128]{2,1,0:T(8,128)S(1)}, u32[]{:S(2)}, u32[]{:S(2)}) collective-permute-start(f32[1,128,128]{2,1,0:T(8,128)S(1)} %get-tuple-element.403), channel_id=1, source_target_pairs={{1,0},{2,1},{3,2},{4,3},{5,4},{6,5},{7,6},{9,8},{10,9},{11,10},{12... | collective-permute-start | bytes 196616 | tf_op jit(solution)/shard_map/while/body/eval_jaxpr/ppermute | solution.py:20
  64.0 12.8 %collective-permute-start = (f32[1,128,128]{2,1,0:T(8,128)S(1)}, f32[1,128,128]{2,1,0:T(8,128)S(1)}, u32[]{:S(2)}, u32[]{:S(2)}) collective-permute-start(f32[1,128,128]{2,1,0:T(8,128)S(1)} %get-tuple-element.403), channel_id=1, source_target_pairs={{1,0},{2,1},{3,2},{4,3},{5,4},{6,5},{7,6},{9,8},{10,9},{11,10},{12... | collective-permute-start | bytes 196616 | tf_op jit(solution)/shard_map/while/body/eval_jaxpr/ppermute | solution.py:20
  90.3 12.8 %collective-permute-start = (f32[1,128,128]{2,1,0:T(8,128)S(1)}, f32[1,128,128]{2,1,0:T(8,128)S(1)}, u32[]{:S(2)}, u32[]{:S(2)}) collective-permute-start(f32[1,128,128]{2,1,0:T(8,128)S(1)} %get-tuple-element.403), channel_id=1, source_target_pairs={{1,0},{2,1},{3,2},{4,3},{5,4},{6,5},{7,6},{9,8},{10,9},{11,10},{12... | collective-permute-start | bytes 196616 | tf_op jit(solution)/shard_map/while/body/eval_jaxpr/ppermute | solution.py:20
  116.6 12.8 %collective-permute-start = (f32[1,128,128]{2,1,0:T(8,128)S(1)}, f32[1,128,128]{2,1,0:T(8,128)S(1)}, u32[]{:S(2)}, u32[]{:S(2)}) collective-permute-start(f32[1,128,128]{2,1,0:T(8,128)S(1)} %get-tuple-element.403), channel_id=1, source_target_pairs={{1,0},{2,1},{3,2},{4,3},{5,4},{6,5},{7,6},{9,8},{10,9},{11,10},{12... | collective-permute-start | bytes 196616 | tf_op jit(solution)/shard_map/while/body/eval_jaxpr/ppermute | solution.py:20
  142.9 12.8 %collective-permute-start = (f32[1,128,128]{2,1,0:T(8,128)S(1)}, f32[1,128,128]{2,1,0:T(8,128)S(1)}, u32[]{:S(2)}, u32[]{:S(2)}) collective-permute-start(f32[1,128,128]{2,1,0:T(8,128)S(1)} %get-tuple-element.403), channel_id=1, source_target_pairs={{1,0},{2,1},{3,2},{4,3},{5,4},{6,5},{7,6},{9,8},{10,9},{11,10},{12... | collective-permute-start | bytes 196616 | tf_op jit(solution)/shard_map/while/body/eval_jaxpr/ppermute | solution.py:20
  169.3 12.8 %collective-permute-start = (f32[1,128,128]{2,1,0:T(8,128)S(1)}, f32[1,128,128]{2,1,0:T(8,128)S(1)}, u32[]{:S(2)}, u32[]{:S(2)}) collective-permute-start(f32[1,128,128]{2,1,0:T(8,128)S(1)} %get-tuple-element.403), channel_id=1, source_target_pairs={{1,0},{2,1},{3,2},{4,3},{5,4},{6,5},{7,6},{9,8},{10,9},{11,10},{12... | collective-permute-start | bytes 196616 | tf_op jit(solution)/shard_map/while/body/eval_jaxpr/ppermute | solution.py:20
  195.6 12.8 %collective-permute-start = (f32[1,128,128]{2,1,0:T(8,128)S(1)}, f32[1,128,128]{2,1,0:T(8,128)S(1)}, u32[]{:S(2)}, u32[]{:S(2)}) collective-permute-start(f32[1,128,128]{2,1,0:T(8,128)S(1)} %get-tuple-element.403), channel_id=1, source_target_pairs={{1,0},{2,1},{3,2},{4,3},{5,4},{6,5},{7,6},{9,8},{10,9},{11,10},{12... | collective-permute-start | bytes 196616 | tf_op jit(solution)/shard_map/while/body/eval_jaxpr/ppermute | solution.py:20
  221.9 12.8 %collective-permute-start = (f32[1,128,128]{2,1,0:T(8,128)S(1)}, f32[1,128,128]{2,1,0:T(8,128)S(1)}, u32[]{:S(2)}, u32[]{:S(2)}) collective-permute-start(f32[1,128,128]{2,1,0:T(8,128)S(1)} %get-tuple-element.403), channel_id=1, source_target_pairs={{1,0},{2,1},{3,2},{4,3},{5,4},{6,5},{7,6},{9,8},{10,9},{11,10},{12... | collective-permute-start | bytes 196616 | tf_op jit(solution)/shard_map/while/body/eval_jaxpr/ppermute | solution.py:20
  248.3 12.8 %collective-permute-start = (f32[1,128,128]{2,1,0:T(8,128)S(1)}, f32[1,128,128]{2,1,0:T(8,128)S(1)}, u32[]{:S(2)}, u32[]{:S(2)}) collective-permute-start(f32[1,128,128]{2,1,0:T(8,128)S(1)} %get-tuple-element.403), channel_id=1, source_target_pairs={{1,0},{2,1},{3,2},{4,3},{5,4},{6,5},{7,6},{9,8},{10,9},{11,10},{12... | collective-permute-start | bytes 196616 | tf_op jit(solution)/shard_map/while/body/eval_jaxpr/ppermute | solution.py:20
  274.6 12.8 %collective-permute-start = (f32[1,128,128]{2,1,0:T(8,128)S(1)}, f32[1,128,128]{2,1,0:T(8,128)S(1)}, u32[]{:S(2)}, u32[]{:S(2)}) collective-permute-start(f32[1,128,128]{2,1,0:T(8,128)S(1)} %get-tuple-element.403), channel_id=1, source_target_pairs={{1,0},{2,1},{3,2},{4,3},{5,4},{6,5},{7,6},{9,8},{10,9},{11,10},{12... | collective-permute-start | bytes 196616 | tf_op jit(solution)/shard_map/while/body/eval_jaxpr/ppermute | solution.py:20
  300.9 12.8 %collective-permute-start = (f32[1,128,128]{2,1,0:T(8,128)S(1)}, f32[1,128,128]{2,1,0:T(8,128)S(1)}, u32[]{:S(2)}, u32[]{:S(2)}) collective-permute-start(f32[1,128,128]{2,1,0:T(8,128)S(1)} %get-tuple-element.403), channel_id=1, source_target_pairs={{1,0},{2,1},{3,2},{4,3},{5,4},{6,5},{7,6},{9,8},{10,9},{11,10},{12... | collective-permute-start | bytes 196616 | tf_op jit(solution)/shard_map/while/body/eval_jaxpr/ppermute | solution.py:20
  327.1 12.8 %collective-permute-start = (f32[1,128,128]{2,1,0:T(8,128)S(1)}, f32[1,128,128]{2,1,0:T(8,128)S(1)}, u32[]{:S(2)}, u32[]{:S(2)}) collective-permute-start(f32[1,128,128]{2,1,0:T(8,128)S(1)} %get-tuple-element.403), channel_id=1, source_target_pairs={{1,0},{2,1},{3,2},{4,3},{5,4},{6,5},{7,6},{9,8},{10,9},{11,10},{12... | collective-permute-start | bytes 196616 | tf_op jit(solution)/shard_map/while/body/eval_jaxpr/ppermute | solution.py:20
  353.5 12.8 %collective-permute-start = (f32[1,128,128]{2,1,0:T(8,128)S(1)}, f32[1,128,128]{2,1,0:T(8,128)S(1)}, u32[]{:S(2)}, u32[]{:S(2)}) collective-permute-start(f32[1,128,128]{2,1,0:T(8,128)S(1)} %get-tuple-element.403), channel_id=1, source_target_pairs={{1,0},{2,1},{3,2},{4,3},{5,4},{6,5},{7,6},{9,8},{10,9},{11,10},{12... | collective-permute-start | bytes 196616 | tf_op jit(solution)/shard_map/while/body/eval_jaxpr/ppermute | solution.py:20
  379.8 12.8 %collective-permute-start = (f32[1,128,128]{2,1,0:T(8,128)S(1)}, f32[1,128,128]{2,1,0:T(8,128)S(1)}, u32[]{:S(2)}, u32[]{:S(2)}) collective-permute-start(f32[1,128,128]{2,1,0:T(8,128)S(1)} %get-tuple-element.403), channel_id=1, source_target_pairs={{1,0},{2,1},{3,2},{4,3},{5,4},{6,5},{7,6},{9,8},{10,9},{11,10},{12... | collective-permute-start | bytes 196616 | tf_op jit(solution)/shard_map/while/body/eval_jaxpr/ppermute | solution.py:20
  406.1 12.8 %collective-permute-start = (f32[1,128,128]{2,1,0:T(8,128)S(1)}, f32[1,128,128]{2,1,0:T(8,128)S(1)}, u32[]{:S(2)}, u32[]{:S(2)}) collective-permute-start(f32[1,128,128]{2,1,0:T(8,128)S(1)} %get-tuple-element.403), channel_id=1, source_target_pairs={{1,0},{2,1},{3,2},{4,3},{5,4},{6,5},{7,6},{9,8},{10,9},{11,10},{12... | collective-permute-start | bytes 196616 | tf_op jit(solution)/shard_map/while/body/eval_jaxpr/ppermute | solution.py:20
  442.6 10.3 %collective-permute-start.10 = (f32[1,128,128]{2,1,0:T(8,128)}, f32[1,128,128]{2,1,0:T(8,128)S(1)}, u32[]{:S(2)}, u32[]{:S(2)}) collective-permute-start(f32[1,128,128]{2,1,0:T(8,128)} %get-tuple-element.297), channel_id=1, source_target_pairs={{1,0},{2,1},{3,2},{4,3},{5,4},{6,5},{7,6},{9,8},{10,9},{11,10},{12... | collective-permute-start | bytes 196616 | tf_op jit(solution)/shard_map/ppermute | solution.py:20
  527.2 13.2 %collective-permute-start.4 = (f32[1,128,128]{2,1,0:T(8,128)}, f32[1,128,128]{2,1,0:T(8,128)S(1)}, u32[]{:S(2)}, u32[]{:S(2)}) collective-permute-start(f32[1,128,128]{2,1,0:T(8,128)} %get-tuple-element.416), channel_id=1, source_target_pairs={{1,0},{2,1},{3,2},{4,3},{5,4},{6,5},{7,6},{9,8},{10,9},{11,10},{12... | collective-permute-start | bytes 196616 | tf_op jit(solution)/shard_map/while/body/eval_jaxpr/ppermute | solution.py:20
  557.0 12.5 %collective-permute-start.4 = (f32[1,128,128]{2,1,0:T(8,128)}, f32[1,128,128]{2,1,0:T(8,128)S(1)}, u32[]{:S(2)}, u32[]{:S(2)}) collective-permute-start(f32[1,128,128]{2,1,0:T(8,128)} %get-tuple-element.416), channel_id=1, source_target_pairs={{1,0},{2,1},{3,2},{4,3},{5,4},{6,5},{7,6},{9,8},{10,9},{11,10},{12... | collective-permute-start | bytes 196616 | tf_op jit(solution)/shard_map/while/body/eval_jaxpr/ppermute | solution.py:20
  586.0 12.5 %collective-permute-start.4 = (f32[1,128,128]{2,1,0:T(8,128)}, f32[1,128,128]{2,1,0:T(8,128)S(1)}, u32[]{:S(2)}, u32[]{:S(2)}) collective-permute-start(f32[1,128,128]{2,1,0:T(8,128)} %get-tuple-element.416), channel_id=1, source_target_pairs={{1,0},{2,1},{3,2},{4,3},{5,4},{6,5},{7,6},{9,8},{10,9},{11,10},{12... | collective-permute-start | bytes 196616 | tf_op jit(solution)/shard_map/while/body/eval_jaxpr/ppermute | solution.py:20
  615.0 12.5 %collective-permute-start.4 = (f32[1,128,128]{2,1,0:T(8,128)}, f32[1,128,128]{2,1,0:T(8,128)S(1)}, u32[]{:S(2)}, u32[]{:S(2)}) collective-permute-start(f32[1,128,128]{2,1,0:T(8,128)} %get-tuple-element.416), channel_id=1, source_target_pairs={{1,0},{2,1},{3,2},{4,3},{5,4},{6,5},{7,6},{9,8},{10,9},{11,10},{12... | collective-permute-start | bytes 196616 | tf_op jit(solution)/shard_map/while/body/eval_jaxpr/ppermute | solution.py:20
  644.0 12.5 %collective-permute-start.4 = (f32[1,128,128]{2,1,0:T(8,128)}, f32[1,128,128]{2,1,0:T(8,128)S(1)}, u32[]{:S(2)}, u32[]{:S(2)}) collective-permute-start(f32[1,128,128]{2,1,0:T(8,128)} %get-tuple-element.416), channel_id=1, source_target_pairs={{1,0},{2,1},{3,2},{4,3},{5,4},{6,5},{7,6},{9,8},{10,9},{11,10},{12... | collective-permute-start | bytes 196616 | tf_op jit(solution)/shard_map/while/body/eval_jaxpr/ppermute | solution.py:20
  673.0 12.5 %collective-permute-start.4 = (f32[1,128,128]{2,1,0:T(8,128)}, f32[1,128,128]{2,1,0:T(8,128)S(1)}, u32[]{:S(2)}, u32[]{:S(2)}) collective-permute-start(f32[1,128,128]{2,1,0:T(8,128)} %get-tuple-element.416), channel_id=1, source_target_pairs={{1,0},{2,1},{3,2},{4,3},{5,4},{6,5},{7,6},{9,8},{10,9},{11,10},{12... | collective-permute-start | bytes 196616 | tf_op jit(solution)/shard_map/while/body/eval_jaxpr/ppermute | solution.py:20
  702.0 12.5 %collective-permute-start.4 = (f32[1,128,128]{2,1,0:T(8,128)}, f32[1,128,128]{2,1,0:T(8,128)S(1)}, u32[]{:S(2)}, u32[]{:S(2)}) collective-permute-start(f32[1,128,128]{2,1,0:T(8,128)} %get-tuple-element.416), channel_id=1, source_target_pairs={{1,0},{2,1},{3,2},{4,3},{5,4},{6,5},{7,6},{9,8},{10,9},{11,10},{12... | collective-permute-start | bytes 196616 | tf_op jit(solution)/shard_map/while/body/eval_jaxpr/ppermute | solution.py:20
  731.0 12.5 %collective-permute-start.4 = (f32[1,128,128]{2,1,0:T(8,128)}, f32[1,128,128]{2,1,0:T(8,128)S(1)}, u32[]{:S(2)}, u32[]{:S(2)}) collective-permute-start(f32[1,128,128]{2,1,0:T(8,128)} %get-tuple-element.416), channel_id=1, source_target_pairs={{1,0},{2,1},{3,2},{4,3},{5,4},{6,5},{7,6},{9,8},{10,9},{11,10},{12... | collective-permute-start | bytes 196616 | tf_op jit(solution)/shard_map/while/body/eval_jaxpr/ppermute | solution.py:20
  760.1 12.5 %collective-permute-start.4 = (f32[1,128,128]{2,1,0:T(8,128)}, f32[1,128,128]{2,1,0:T(8,128)S(1)}, u32[]{:S(2)}, u32[]{:S(2)}) collective-permute-start(f32[1,128,128]{2,1,0:T(8,128)} %get-tuple-element.416), channel_id=1, source_target_pairs={{1,0},{2,1},{3,2},{4,3},{5,4},{6,5},{7,6},{9,8},{10,9},{11,10},{12... | collective-permute-start | bytes 196616 | tf_op jit(solution)/shard_map/while/body/eval_jaxpr/ppermute | solution.py:20
  789.1 12.5 %collective-permute-start.4 = (f32[1,128,128]{2,1,0:T(8,128)}, f32[1,128,128]{2,1,0:T(8,128)S(1)}, u32[]{:S(2)}, u32[]{:S(2)}) collective-permute-start(f32[1,128,128]{2,1,0:T(8,128)} %get-tuple-element.416), channel_id=1, source_target_pairs={{1,0},{2,1},{3,2},{4,3},{5,4},{6,5},{7,6},{9,8},{10,9},{11,10},{12... | collective-permute-start | bytes 196616 | tf_op jit(solution)/shard_map/while/body/eval_jaxpr/ppermute | solution.py:20
  818.1 12.5 %collective-permute-start.4 = (f32[1,128,128]{2,1,0:T(8,128)}, f32[1,128,128]{2,1,0:T(8,128)S(1)}, u32[]{:S(2)}, u32[]{:S(2)}) collective-permute-start(f32[1,128,128]{2,1,0:T(8,128)} %get-tuple-element.416), channel_id=1, source_target_pairs={{1,0},{2,1},{3,2},{4,3},{5,4},{6,5},{7,6},{9,8},{10,9},{11,10},{12... | collective-permute-start | bytes 196616 | tf_op jit(solution)/shard_map/while/body/eval_jaxpr/ppermute | solution.py:20
  847.1 12.5 %collective-permute-start.4 = (f32[1,128,128]{2,1,0:T(8,128)}, f32[1,128,128]{2,1,0:T(8,128)S(1)}, u32[]{:S(2)}, u32[]{:S(2)}) collective-permute-start(f32[1,128,128]{2,1,0:T(8,128)} %get-tuple-element.416), channel_id=1, source_target_pairs={{1,0},{2,1},{3,2},{4,3},{5,4},{6,5},{7,6},{9,8},{10,9},{11,10},{12... | collective-permute-start | bytes 196616 | tf_op jit(solution)/shard_map/while/body/eval_jaxpr/ppermute | solution.py:20
  876.1 12.5 %collective-permute-start.4 = (f32[1,128,128]{2,1,0:T(8,128)}, f32[1,128,128]{2,1,0:T(8,128)S(1)}, u32[]{:S(2)}, u32[]{:S(2)}) collective-permute-start(f32[1,128,128]{2,1,0:T(8,128)} %get-tuple-element.416), channel_id=1, source_target_pairs={{1,0},{2,1},{3,2},{4,3},{5,4},{6,5},{7,6},{9,8},{10,9},{11,10},{12... | collective-permute-start | bytes 196616 | tf_op jit(solution)/shard_map/while/body/eval_jaxpr/ppermute | solution.py:20
  905.2 12.5 %collective-permute-start.4 = (f32[1,128,128]{2,1,0:T(8,128)}, f32[1,128,128]{2,1,0:T(8,128)S(1)}, u32[]{:S(2)}, u32[]{:S(2)}) collective-permute-start(f32[1,128,128]{2,1,0:T(8,128)} %get-tuple-element.416), channel_id=1, source_target_pairs={{1,0},{2,1},{3,2},{4,3},{5,4},{6,5},{7,6},{9,8},{10,9},{11,10},{12... | collective-permute-start | bytes 196616 | tf_op jit(solution)/shard_map/while/body/eval_jaxpr/ppermute | solution.py:20
  934.1 12.5 %collective-permute-start.4 = (f32[1,128,128]{2,1,0:T(8,128)}, f32[1,128,128]{2,1,0:T(8,128)S(1)}, u32[]{:S(2)}, u32[]{:S(2)}) collective-permute-start(f32[1,128,128]{2,1,0:T(8,128)} %get-tuple-element.416), channel_id=1, source_target_pairs={{1,0},{2,1},{3,2},{4,3},{5,4},{6,5},{7,6},{9,8},{10,9},{11,10},{12... | collective-permute-start | bytes 196616 | tf_op jit(solution)/shard_map/while/body/eval_jaxpr/ppermute | solution.py:20
  (148 other events, 1292.4 us)
where the time goes:
time: 981 us; the launch traced here: 966 us
  starting transfers between devices  407 us (41%)
  other arithmetic  202 us (21%)
  loops' own time  135 us (14%)
  local copies, waits for them, and re-layouts  131 us (13%)
  waiting for transfers between devices  88.6 us (9%)
    ppermute x68, starting transfers between devices, padded_2(): after = lax.ppermute(initial, axis, down)  202 us
    ppermute x68, starting transfers between devices, padded_2(): before = lax.ppermute(last, axis, up)  199 us
    div x50, other arithmetic, jacobi_sweep(): return summed / (1.0 + 6.0 * diffusion)  92.3 us
    another operation x1, loops' own time, local(): lax.scan(second_pass, second_state, jnp.arange(steps_dev - 1))  67.6 us
    another operation x1, loops' own time, local(): lax.scan(first_pass, first_state, jnp.arange(steps_dev))  67 us
    concatenate x68, other arithmetic, padded_2(): x = jnp.concatenate([before, x, after], axis=dim)  63.9 us
    ppermute x68, waiting for transfers between devices, padded_2(): before = lax.ppermute(last, axis, up)  48.5 us
    slice x68, local copies, waits for them, and re-layouts, padded_2(): last = lax.slice_in_dim(x, length - width, length, axis=dim)  48.2 us
  transfers between devices with their start and end apart: 141, of which 56 were waited for; matrix products, arithmetic and copies ran while one was open for 7% of the time, Pallas kernels for 0%

commit v1 on v0

v1 whole, which is shorter than its diff:
```python
import functools

import jax
import jax.numpy as jnp
from jax import lax
from jax.experimental import pallas as pl
from jax.experimental.pallas import tpu as pltpu
from jax.sharding import PartitionSpec as P

PAD = 8
CHUNK = 32
MESH = pl.DeviceIdType.MESH


def padded_1(x):
    peers, length = (lax.axis_size("space"), x.shape[0])
    up = [(i, i + 1) for i in range(peers - 1)]
    down = [(i + 1, i) for i in range(peers - 1)]
    before = lax.ppermute(x[length - 1 :], "space", up)
    after = lax.ppermute(x[:1], "space", down)
    return jnp.concatenate([before, x, after], axis=0)


def kernel(
    blocks, slabs, fan, initial, guess, velocity, heat, states,
    cur, mid, inc, start, own_guess, residual, corr, vel,
    halo_send, halo_recv, inc_send, inc_recv, vel_send, vel_recv,
    tm_send, tm_recv, local_sem,
):
    steps = states.shape[0]
    planes, ny, nz = initial.shape
    rows = pl.ds(PAD, ny)
    k = lax.axis_index("tm")
    j = lax.axis_index("space")
    has_left, has_right = j > 0, j < slabs - 1
    has_before, has_after = k > 0, k < blocks - 1
    sides = ((0, has_left, j - 1), (1, has_right, j + 1))

    cur[...] = jnp.zeros_like(cur)
    mid[...] = jnp.zeros_like(mid)
    inc[...] = jnp.zeros_like(inc)
    for edge in (0, planes + 1):
        for mode in range(vel.shape[0]):
            vel[mode, :, edge] = jnp.zeros((3, ny, nz), jnp.float32)

    barrier = pltpu.get_barrier_semaphore()
    greet = (
        (has_left, {"space": j - 1}), (has_right, {"space": j + 1}),
        (has_before, {"tm": k - 1}), (has_after, {"tm": k + 1}),
    )
    for there, who in greet:
        @pl.when(there)
        def _():
            pl.semaphore_signal(barrier, inc=1, device_id=who, device_id_type=MESH)
    pl.semaphore_wait(barrier, sum(there.astype(jnp.int32) for there, who in greet))

    def edges_of(side, width, first):
        if side == 0:
            return pl.ds(first, width), pl.ds(first + planes, width)
        return pl.ds(first + planes - width, width), pl.ds(first - width, width)

    def edge_copy(side, peer, buffer, send, recv):
        here, there = edges_of(side, 2, 2)
        return pltpu.make_async_remote_copy(
            src_ref=buffer.at[here, rows], dst_ref=buffer.at[there, rows],
            send_sem=send, recv_sem=recv,
            device_id={"space": peer}, device_id_type=MESH,
        )

    def vel_copy(side, peer):
        here, there = edges_of(side, 1, 1)
        here = pl.ds(0, 1) if side == 0 else pl.ds(planes - 1, 1)
        return pltpu.make_async_remote_copy(
            src_ref=velocity.at[:, :, here], dst_ref=vel.at[:, :, there],
            send_sem=vel_send.at[side], recv_sem=vel_recv.at[1 - side],
            device_id={"space": peer}, device_id_type=MESH,
        )

    def both(copy_of, act):
        for side, there, peer in sides:
            @pl.when(there)
            def _():
                act(side, copy_of(side, peer))

    def begin(side, copy):
        copy.start()

    def end(recv_of):
        def act(side, copy):
            copy.wait_send()
        return act

    own = pl.ds(2, planes)
    guess_copy = pltpu.make_async_remote_copy(
        src_ref=guess.at[0], dst_ref=cur.at[0, own, rows],
        send_sem=tm_send.at[0], recv_sem=tm_recv.at[0],
        device_id={"tm": k + 1}, device_id_type=MESH,
    )
    corr_copy = pltpu.make_async_remote_copy(
        src_ref=corr, dst_ref=inc.at[own, rows],
        send_sem=tm_send.at[1], recv_sem=tm_recv.at[1],
        device_id={"tm": k + 1}, device_id_type=MESH,
    )

    @pl.when(has_after)
    def _():
        guess_copy.start()

    both(vel_copy, begin)
    vel_in = pltpu.make_async_copy(velocity, vel.at[:, :, pl.ds(1, planes)], local_sem.at[0])
    vel_in.start()
    guess_in = pltpu.make_async_copy(guess.at[0], own_guess, local_sem.at[1])
    guess_in.start()

    @pl.when(jnp.logical_not(has_before))
    def _():
        first_in = pltpu.make_async_copy(initial, cur.at[0, own, rows], local_sem.at[2])
        first_in.start()
        first_in.wait()

    @pl.when(has_before)
    def _():
        guess_copy.wait_recv()

    def cur_copy(slot):
        def make(side, peer):
            return edge_copy(
                side, peer, cur.at[slot], halo_send.at[slot, side], halo_recv.at[slot, 1 - side]
            )
        return make

    def inc_copy(side, peer):
        return edge_copy(side, peer, inc, inc_send.at[side], inc_recv.at[1 - side])

    def wait_edges(make):
        for side, there, peer in sides:
            @pl.when(there)
            def _():
                make(side, peer).wait_send()
                make(1 - side, peer).wait_recv()

    both(cur_copy(0), begin)
    vel_in.wait()
    guess_in.wait()
    for side, there, peer in sides:
        @pl.when(there)
        def _():
            vel_copy(side, peer).wait_send()
            vel_copy(1 - side, peer).wait_recv()
    wait_edges(cur_copy(0))

    lane = lax.broadcasted_iota(jnp.int32, (CHUNK, nz), 1)
    low, high = lane == 0, lane == nz - 1

    def sweep(read, source, fan_index, vel_plane, ratio, scale, store):
        half = 0.5 * ratio
        for at in range(0, ny, CHUNK):
            here = pl.ds(PAD + at, CHUNK)
            tile = pl.ds(at, CHUNK)
            centre = read(1, here)
            after, before = read(2, here), read(0, here)
            total = after + before
            drift = vel[fan_index, 0, vel_plane, tile] * (after - before)
            after = read(1, pl.ds(PAD + at + 1, CHUNK))
            before = read(1, pl.ds(PAD + at - 1, CHUNK))
            total = total + (after + before)
            drift = drift + vel[fan_index, 1, vel_plane, tile] * (after - before)
            after = jnp.where(high, 0.0, pltpu.roll(centre, nz - 1, 1))
            before = jnp.where(low, 0.0, pltpu.roll(centre, 1, 1))
            total = total + (after + before)
            drift = drift + vel[fan_index, 2, vel_plane, tile] * (after - before)
            store(tile, here, (source(tile, here) + half * (total - drift)) * scale)

    def first_sweep(wide, fan_index, ratio, heat_of):
        inverse = 1.0 / (1.0 + 3.0 * ratio)

        def plane(i, carry):
            off = jnp.logical_or(
                jnp.logical_and(i == 0, j == 0),
                jnp.logical_and(i == planes + 1, j == slabs - 1),
            )
            scale = jnp.where(off, 0.0, inverse).astype(jnp.float32)

            def source(tile, here):
                value = wide[i + 1, here]
                return value if heat_of is None else value + heat_of(i, tile)

            def store(tile, here, value):
                mid[i, here] = value

            sweep(lambda d, at: wide[i + d, at], source, fan_index, i, ratio, scale, store)
            return carry

        lax.fori_loop(0, planes + 2, plane, 0)

    def second_sweep(wide, fan_index, ratio, heat_of, put):
        inverse = 1.0 / (1.0 + 3.0 * ratio)

        def plane(i, carry):
            def source(tile, here):
                value = wide[i + 2, here]
                return value if heat_of is None else value + heat_of(i + 1, tile)

            sweep(
                lambda d, at: mid[i + d, at], source, fan_index, i + 1, ratio, inverse,
                lambda tile, here, value: put(i, tile, here, value),
            )
            return carry

        lax.fori_loop(0, planes, plane, 0)

    def step(s, keep, more):
        slot = lax.rem(s, 2)
        other = 1 - slot

        @pl.when(s > 0)
        def _():
            wait_edges(cur_copy(slot))

        fan_index = fan[k * steps + s]
        wide = cur.at[slot]

        def heat_of(i, tile):
            return heat[s, i, tile]

        def put(i, tile, here, value):
            cur[other, i + 2, here] = value
            if keep:
                states[s, i, tile] = value

        first_sweep(wide, fan_index, 1.0, heat_of)
        second_sweep(wide, fan_index, 1.0, heat_of, put)

        @pl.when(more)
        def _():
            both(cur_copy(other), begin)

    start[...] = cur[0]

    def pass_one(s, carry):
        step(s, False, s < steps - 1)
        return carry

    lax.fori_loop(0, steps, pass_one, 0)
    for i in range(planes):
        residual[i] = cur[steps % 2, i + 2, rows] - own_guess[i]

    @pl.when(has_before)
    def _():
        corr_copy.wait_recv()

    both(inc_copy, begin)
    wait_edges(inc_copy)

    coarse_fan = fan[k * steps + steps - 1]
    coarse = float(steps)

    def put_corr(i, tile, here, value):
        value = value + residual[i, tile]
        corr[i, tile] = value
        states[steps - 1, i, tile] = own_guess[i, tile] + value

    first_sweep(inc, coarse_fan, coarse, None)
    second_sweep(inc, coarse_fan, coarse, None, put_corr)

    @pl.when(has_after)
    def _():
        corr_copy.start()

    cur[0] = start[...] + inc[...]

    def pass_two(s, carry):
        step(s, True, s < steps - 2)
        return carry

    lax.fori_loop(0, steps - 1, pass_two, 0)

    @pl.when(has_after)
    def _():
        guess_copy.wait_send()
        corr_copy.wait_send()


def local(initial, guess, velocity, heat_shape, rack_map, power, fan_mode):
    blocks, slabs = lax.axis_size("tm"), lax.axis_size("space")
    planes, ny, nz = initial.shape
    steps, racks = power.shape
    rack_wide = padded_1(rack_map)
    heat_wide = padded_1(heat_shape)
    onehot = (rack_wide[:, :, None] == lax.iota(jnp.int32, racks)[None, None, :]).astype(jnp.float32)
    cell_power = jnp.einsum(
        "xyr,kr->kxy", onehot, power.astype(jnp.float32), precision=lax.Precision.HIGHEST
    )
    heat = heat_wide[None] * cell_power[:, :, :, None]
    tall = ny + 2 * PAD
    vmem = pl.BlockSpec(memory_space=pltpu.VMEM)
    hbm = pl.BlockSpec(memory_space=pl.ANY)
    f32 = jnp.float32
    return pl.pallas_call(
        functools.partial(kernel, blocks, slabs),
        out_shape=jax.ShapeDtypeStruct((steps, planes, ny, nz), f32),
        in_specs=[pl.BlockSpec(memory_space=pltpu.SMEM), hbm, hbm, hbm, vmem],
        out_specs=vmem,
        scratch_shapes=[
            pltpu.VMEM((2, planes + 4, tall, nz), f32),
            pltpu.VMEM((planes + 2, tall, nz), f32),
            pltpu.VMEM((planes + 4, tall, nz), f32),
            pltpu.VMEM((planes + 4, tall, nz), f32),
            pltpu.VMEM((planes, ny, nz), f32),
            pltpu.VMEM((planes, ny, nz), f32),
            pltpu.VMEM((planes, ny, nz), f32),
            pltpu.VMEM((velocity.shape[0], 3, planes + 2, ny, nz), f32),
            pltpu.SemaphoreType.DMA((2, 2)),
            pltpu.SemaphoreType.DMA((2, 2)),
            pltpu.SemaphoreType.DMA((2,)),
            pltpu.SemaphoreType.DMA((2,)),
            pltpu.SemaphoreType.DMA((2,)),
            pltpu.SemaphoreType.DMA((2,)),
            pltpu.SemaphoreType.DMA((2,)),
            pltpu.SemaphoreType.DMA((2,)),
            pltpu.SemaphoreType.DMA((3,)),
        ],
        compiler_params=pltpu.CompilerParams(
            collective_id=0, has_side_effects=True, vmem_limit_bytes=40 * 1024 * 1024
        ),
    )(fan_mode, initial, guess, velocity, heat)


def solution(mesh):
    placed = (
        P("space", None, None),
        P("tm", "space", None, None),
        P(None, None, "space", None, None),
        P("space", None, None),
        P("space", None),
        P("tm", None),
        P(),
    )
    return jax.shard_map(
        local, mesh=mesh, in_specs=placed, out_specs=P("tm", "space", None, None), check_vma=False
    )
```

time: 981 us -> 213 us (0.22); the launches traced: 966 us -> 213 us
  starting transfers between devices: 407 us -> 11.4 us
  other arithmetic: 202 us -> 3.46 us
  Pallas kernels: 0 us -> 191 us
  loops' own time: 135 us -> 0 us
  local copies, waits for them, and re-layouts: 131 us -> 3.79 us
  waiting for transfers between devices: 88.6 us -> 2.04 us
    ppermute x141 -> x4, starting transfers between devices: 407 us -> 11.4 us  [the longest x2 7.53 us: padded_1(): before = lax.ppermute(x[length - 1:], 'space', up)]
    pallas_call x0 -> x1, Pallas kernels: none -> 191 us  [local(): pl.pallas_call(functools.partial(kernel, blocks, slabs), out_shape=jax.Sh...]
    another operation x2 -> x0, loops' own time: 135 us -> none  [the longest x1 67.6 us: local(): lax.scan(second_pass, second_state, jnp.arange(steps_dev - 1))]
    div x50 -> x0, other arithmetic: 92.3 us -> none  [jacobi_sweep(): return summed / (1.0 + 6.0 * diffusion)]
    ppermute x141 -> x4, waiting for transfers between devices: 88.6 us -> 2.04 us  [the longest x2 2.03 us: padded_1(): after = lax.ppermute(x[:1], 'space', down)]
    concatenate x69 -> x2, other arithmetic: 68.6 us -> 1.67 us  [padded_1(): return jnp.concatenate([before, x, after], axis=0)]
    dynamic_slice x63 -> x0, local copies, waits for them, and re-layouts: 49.5 us -> none  [the longest x31 30 us: advance(): lax.dynamic_index_in_dim(fan_mode, block_index * steps_dev + step_index,...]
    slice x68 -> x2, local copies, waits for them, and re-layouts: 48.2 us -> 1.74 us  [padded_1(): before = lax.ppermute(x[length - 1:], 'space', up)]
  transfers between devices with their start and end apart: 141 -> 4, of which waited for: 56 -> 1; matrix products, arithmetic and copies ran while one was open for 7% -> 1% of each run, Pallas kernels for 0% -> 0%
where the time goes in v1:
time: 213 us
  Pallas kernels  191 us (90%)
  starting transfers between devices  11.4 us (5%)
  local copies, waits for them, and re-layouts  3.79 us (2%)
  other arithmetic  3.46 us (2%)
    pallas_call x1, Pallas kernels, local(): pl.pallas_call(functools.partial(kernel, blocks, slabs), out_shape=jax.Sh...  191 us
    ppermute x2, starting transfers between devices, padded_1(): before = lax.ppermute(x[length - 1:], 'space', up)  7.53 us
  transfers between devices with their start and end apart: 4, of which 1 were waited for; matrix products, arithmetic and copies ran while one was open for 1% of the time, Pallas kernels for 0%

profile of v1, /device:TPU:15, one launch (start us, length us, event | category | flops | bytes accessed | tf_op | source)
XLA Modules:
  0.0 212.6 jit_solution(1163488770163467674)
XLA Ops:
  0.0 0.0 copy-start.3
  0.0 0.0 copy-start
  0.0 0.0 copy-start.2
  0.0 0.0 copy-start.1
  0.0 0.9 fusion.4
  0.9 3.9 %collective-permute-start.2 = (s32[1,128]{1,0:T(1,128)S(1)}, s32[1,128]{1,0:T(1,128)S(1)}, u32[]{:S(2)}, u32[]{:S(2)}) collective-permute-start(s32[1,128]{1,0:T(1,128)S(1)} %get-tuple-element.7), channel_id=1, source_target_pairs={{0,1},{1,2},{2,3},{3,4},{4,5},{5,6},{6,7},{8,9},{9,10},{10,11},{11... | collective-permute-start | bytes 1544 | tf_op jit(solution)/shard_map/ppermute | solution.py:19
  4.8 1.9 collective-permute-start.3
  6.7 0.9 fusion.3
  7.6 3.6 %collective-permute-start = (f32[1,128,128]{2,1,0:T(8,128)S(1)}, f32[1,128,128]{2,1,0:T(8,128)S(1)}, u32[]{:S(2)}, u32[]{:S(2)}) collective-permute-start(f32[1,128,128]{2,1,0:T(8,128)S(1)} %get-tuple-element.5), channel_id=1, source_target_pairs={{0,1},{1,2},{2,3},{3,4},{4,5},{5,6},{6,7},{8,9},{9,10},{10,11},{11... | collective-permute-start | bytes 196616 | tf_op jit(solution)/shard_map/ppermute | solution.py:19
  11.2 1.9 collective-permute-start.1
  13.2 0.0 collective-permute-done.2
  13.2 0.0 collective-permute-done.3
  13.2 0.7 pad_add_fusion
  13.9 0.9 convolution_bitcast_fusion
  14.8 0.0 collective-permute-done
  14.8 2.0 collective-permute-done.1
  16.8 1.0 pad_maximum_fusion
  17.8 1.8 broadcast_multiply_fusion.heat
  19.6 0.0 copy-done.3
  19.6 0.0 copy-done
  19.6 0.0 copy-done.2
  19.6 0.0 copy-done.1
  19.6 190.9 %shard_map.73 = f32[16,4,128,128]{3,2,1,0:T(8,128)S(1)} custom-call(s32[64]{0:T(128)S(1)} %copy-done.3, f32[4,128,128]{2,1,0:T(8,128)S(1)} %copy-done.1, f32[1,4,128,128]{3,2,1,0:T(8,128)S(1)} %copy-done.2, f32[4,3,4,128,128]{4,3,2,1,0:T(8,128)S(1)} %copy-done, f32[16,6,128,128]{3,2,1,0:T(8,128)S(1)} %broadcast_multiply_fusion.heat), custom_call_target="tpu_custom_call" | custom-call | tf_op jit(solution)/shard_map/pallas_call | solution.py:299
  210.6 2.0 copy.10
  (1 shorter events, 0.0 us)
Async XLA Ops:
  0.0 19.6 %copy-start.3 = (s32[64]{0:T(128)S(1)}, s32[64]{0:T(128)}, u32[]{:S(2)}) copy-start(s32[64]{0:T(128)} %fan.1) | copy-start | bytes 772
  0.0 19.6 %copy-start = (f32[4,3,4,128,128]{4,3,2,1,0:T(8,128)S(1)}, f32[4,3,4,128,128]{4,3,2,1,0:T(8,128)}, u32[]{:S(2)}) copy-start(f32[4,3,4,128,128]{4,3,2,1,0:T(8,128)} %velocity.1) | copy-start | bytes 9437188
  0.0 19.6 %copy-start.2 = (f32[1,4,128,128]{3,2,1,0:T(8,128)S(1)}, f32[1,4,128,128]{3,2,1,0:T(8,128)}, u32[]{:S(2)}) copy-start(f32[1,4,128,128]{3,2,1,0:T(8,128)} %guess.1) | copy-start | bytes 786436
  0.0 19.6 %copy-start.1 = (f32[4,128,128]{2,1,0:T(8,128)S(1)}, f32[4,128,128]{2,1,0:T(8,128)}, u32[]{:S(2)}) copy-start(f32[4,128,128]{2,1,0:T(8,128)} %initial.1) | copy-start | bytes 786436
  0.9 12.3 %collective-permute-start.2 = (s32[1,128]{1,0:T(1,128)S(1)}, s32[1,128]{1,0:T(1,128)S(1)}, u32[]{:S(2)}, u32[]{:S(2)}) collective-permute-start(s32[1,128]{1,0:T(1,128)S(1)} %get-tuple-element.7), channel_id=1, source_target_pairs={{0,1},{1,2},{2,3},{3,4},{4,5},{5,6},{6,7},{8,9},{9,10},{10,11},{11... | collective-permute-start | bytes 1544 | tf_op jit(solution)/shard_map/ppermute | solution.py:19
  4.8 8.4 %collective-permute-start.3 = (s32[1,128]{1,0:T(1,128)S(1)}, s32[1,128]{1,0:T(1,128)S(1)}, u32[]{:S(2)}, u32[]{:S(2)}) collective-permute-start(s32[1,128]{1,0:T(1,128)S(1)} %get-tuple-element.8), channel_id=1, source_target_pairs={{1,0},{2,1},{3,2},{4,3},{5,4},{6,5},{7,6},{9,8},{10,9},{11,10},{12... | collective-permute-start | bytes 1544 | tf_op jit(solution)/shard_map/ppermute | solution.py:20
  7.6 7.2 %collective-permute-start = (f32[1,128,128]{2,1,0:T(8,128)S(1)}, f32[1,128,128]{2,1,0:T(8,128)S(1)}, u32[]{:S(2)}, u32[]{:S(2)}) collective-permute-start(f32[1,128,128]{2,1,0:T(8,128)S(1)} %get-tuple-element.5), channel_id=1, source_target_pairs={{0,1},{1,2},{2,3},{3,4},{4,5},{5,6},{6,7},{8,9},{9,10},{10,11},{11... | collective-permute-start | bytes 196616 | tf_op jit(solution)/shard_map/ppermute | solution.py:19
  11.2 5.6 %collective-permute-start.1 = (f32[1,128,128]{2,1,0:T(8,128)S(1)}, f32[1,128,128]{2,1,0:T(8,128)S(1)}, u32[]{:S(2)}, u32[]{:S(2)}) collective-permute-start(f32[1,128,128]{2,1,0:T(8,128)S(1)} %get-tuple-element.6), channel_id=1, source_target_pairs={{1,0},{2,1},{3,2},{4,3},{5,4},{6,5},{7,6},{9,8},{10,9},{11,10},{12... | collective-permute-start | bytes 196616 | tf_op jit(solution)/shard_map/ppermute | solution.py:20

commit v2 on v1

--- a/solution.py
+++ b/solution.py
@@ -8,28 +8,22 @@
 from jax.sharding import PartitionSpec as P
 
 PAD = 8
-CHUNK = 32
+PARTS = 4
 MESH = pl.DeviceIdType.MESH
 
 
-def padded_1(x):
-    peers, length = (lax.axis_size("space"), x.shape[0])
-    up = [(i, i + 1) for i in range(peers - 1)]
-    down = [(i + 1, i) for i in range(peers - 1)]
-    before = lax.ppermute(x[length - 1 :], "space", up)
-    after = lax.ppermute(x[:1], "space", down)
-    return jnp.concatenate([before, x, after], axis=0)
-
-
 def kernel(
-    blocks, slabs, fan, initial, guess, velocity, heat, states,
-    cur, mid, inc, start, own_guess, residual, corr, vel,
+    blocks, slabs, fan, initial, guess, velocity, shape_own, onehot_own, levels, states,
+    heat, shape_wide, onehot, cur, mid, inc, start, own_guess, residual, corr, vel,
     halo_send, halo_recv, inc_send, inc_recv, vel_send, vel_recv,
+    shape_send, shape_recv, onehot_send, onehot_recv,
     tm_send, tm_recv, local_sem,
 ):
     steps = states.shape[0]
     planes, ny, nz = initial.shape
     rows = pl.ds(PAD, ny)
+    chunk = ny // PARTS
+    halves = ((0, pl.ds(PAD, ny // 2)), (1, pl.ds(PAD + ny // 2, ny // 2)))
     k = lax.axis_index("tm")
     j = lax.axis_index("space")
     has_left, has_right = j > 0, j < slabs - 1
@@ -42,6 +36,8 @@
     for edge in (0, planes + 1):
         for mode in range(vel.shape[0]):
             vel[mode, :, edge] = jnp.zeros((3, ny, nz), jnp.float32)
+        shape_wide[edge] = jnp.zeros((ny, nz), jnp.float32)
+        onehot[edge] = jnp.zeros(onehot.shape[1:], jnp.float32)
 
     barrier = pltpu.get_barrier_semaphore()
     greet = (
@@ -59,7 +55,7 @@
             return pl.ds(first, width), pl.ds(first + planes, width)
         return pl.ds(first + planes - width, width), pl.ds(first - width, width)
 
-    def edge_copy(side, peer, buffer, send, recv):
+    def edge_copy(side, peer, buffer, send, recv, rows=rows):
         here, there = edges_of(side, 2, 2)
         return pltpu.make_async_remote_copy(
             src_ref=buffer.at[here, rows], dst_ref=buffer.at[there, rows],
@@ -76,6 +72,20 @@
             device_id={"space": peer}, device_id_type=MESH,
         )
 
+    def plane_copy(source, wide, send, recv):
+        def make(side, peer):
+            here, there = edges_of(side, 1, 1)
+            here = pl.ds(0, 1) if side == 0 else pl.ds(planes - 1, 1)
+            return pltpu.make_async_remote_copy(
+                src_ref=source.at[here], dst_ref=wide.at[there],
+                send_sem=send.at[side], recv_sem=recv.at[1 - side],
+                device_id={"space": peer}, device_id_type=MESH,
+            )
+        return make
+
+    shape_copy = plane_copy(shape_own, shape_wide, shape_send, shape_recv)
+    onehot_copy = plane_copy(onehot_own, onehot, onehot_send, onehot_recv)
+
     def both(copy_of, act):
         for side, there, peer in sides:
             @pl.when(there)
@@ -85,11 +95,6 @@
     def begin(side, copy):
         copy.start()
 
-    def end(recv_of):
-        def act(side, copy):
-            copy.wait_send()
-        return act
-
     own = pl.ds(2, planes)
     guess_copy = pltpu.make_async_remote_copy(
         src_ref=guess.at[0], dst_ref=cur.at[0, own, rows],
@@ -106,12 +111,20 @@
     def _():
         guess_copy.start()
 
+    both(shape_copy, begin)
+    both(onehot_copy, begin)
     both(vel_copy, begin)
     vel_in = pltpu.make_async_copy(velocity, vel.at[:, :, pl.ds(1, planes)], local_sem.at[0])
     vel_in.start()
     guess_in = pltpu.make_async_copy(guess.at[0], own_guess, local_sem.at[1])
     guess_in.start()
 
+    middle = pl.ds(1, planes)
+    shape_in = pltpu.make_async_copy(shape_own, shape_wide.at[middle], local_sem.at[3])
+    shape_in.start()
+    onehot_in = pltpu.make_async_copy(onehot_own, onehot.at[middle], local_sem.at[4])
+    onehot_in.start()
+
     @pl.when(jnp.logical_not(has_before))
     def _():
         first_in = pltpu.make_async_copy(initial, cur.at[0, own, rows], local_sem.at[2])
@@ -122,10 +135,11 @@
     def _():
         guess_copy.wait_recv()
 
-    def cur_copy(slot):
+    def cur_copy(slot, half):
         def make(side, peer):
             return edge_copy(
-                side, peer, cur.at[slot], halo_send.at[slot, side], halo_recv.at[slot, 1 - side]
+                side, peer, cur.at[slot], halo_send.at[slot, side, half],
+                halo_recv.at[slot, 1 - side, half], halves[half][1],
             )
         return make
 
@@ -139,30 +153,40 @@
                 make(side, peer).wait_send()
                 make(1 - side, peer).wait_recv()
 
-    both(cur_copy(0), begin)
+    for half in range(2):
+        both(cur_copy(0, half), begin)
     vel_in.wait()
     guess_in.wait()
-    for side, there, peer in sides:
-        @pl.when(there)
-        def _():
-            vel_copy(side, peer).wait_send()
-            vel_copy(1 - side, peer).wait_recv()
-    wait_edges(cur_copy(0))
-
-    lane = lax.broadcasted_iota(jnp.int32, (CHUNK, nz), 1)
+    shape_in.wait()
+    onehot_in.wait()
+    wait_edges(shape_copy)
+    wait_edges(onehot_copy)
+
+    def heat_step(s, carry):
+        for i in range(planes + 2):
+            picked = jnp.dot(onehot[i], levels[s], preferred_element_type=jnp.float32)
+            heat[s, i] = shape_wide[i] * picked
+        return carry
+
+    lax.fori_loop(0, steps, heat_step, 0)
+    wait_edges(vel_copy)
+    for half in range(2):
+        wait_edges(cur_copy(0, half))
+
+    lane = lax.broadcasted_iota(jnp.int32, (chunk, nz), 1)
     low, high = lane == 0, lane == nz - 1
 
-    def sweep(read, source, fan_index, vel_plane, ratio, scale, store):
+    def sweep(parts, read, source, fan_index, vel_plane, ratio, scale, store):
         half = 0.5 * ratio
-        for at in range(0, ny, CHUNK):
-            here = pl.ds(PAD + at, CHUNK)
-            tile = pl.ds(at, CHUNK)
+        for at in (part * chunk for part in parts):
+            here = pl.ds(PAD + at, chunk)
+            tile = pl.ds(at, chunk)
             centre = read(1, here)
             after, before = read(2, here), read(0, here)
             total = after + before
             drift = vel[fan_index, 0, vel_plane, tile] * (after - before)
-            after = read(1, pl.ds(PAD + at + 1, CHUNK))
-            before = read(1, pl.ds(PAD + at - 1, CHUNK))
+            after = read(1, pl.ds(PAD + at + 1, chunk))
+            before = read(1, pl.ds(PAD + at - 1, chunk))
             total = total + (after + before)
             drift = drift + vel[fan_index, 1, vel_plane, tile] * (after - before)
             after = jnp.where(high, 0.0, pltpu.roll(centre, nz - 1, 1))
@@ -171,10 +195,13 @@
             drift = drift + vel[fan_index, 2, vel_plane, tile] * (after - before)
             store(tile, here, (source(tile, here) + half * (total - drift)) * scale)
 
-    def first_sweep(wide, fan_index, ratio, heat_of):
+    def first_sweep(parts, which, wide, fan_index, ratio, heat_of):
         inverse = 1.0 / (1.0 + 3.0 * ratio)
 
-        def plane(i, carry):
+        count, index_of = which
+
+        def plane(turn, carry):
+            i = index_of(turn)
             off = jnp.logical_or(
                 jnp.logical_and(i == 0, j == 0),
                 jnp.logical_and(i == planes + 1, j == slabs - 1),
@@ -188,12 +215,12 @@
             def store(tile, here, value):
                 mid[i, here] = value
 
-            sweep(lambda d, at: wide[i + d, at], source, fan_index, i, ratio, scale, store)
+            sweep(parts, lambda d, at: wide[i + d, at], source, fan_index, i, ratio, scale, store)
             return carry
 
-        lax.fori_loop(0, planes + 2, plane, 0)
-
-    def second_sweep(wide, fan_index, ratio, heat_of, put):
+        lax.fori_loop(0, count, plane, 0)
+
+    def second_sweep(parts, wide, fan_index, ratio, heat_of, put):
         inverse = 1.0 / (1.0 + 3.0 * ratio)
 
         def plane(i, carry):
@@ -202,20 +229,22 @@
                 return value if heat_of is None else value + heat_of(i + 1, tile)
 
             sweep(
-                lambda d, at: mid[i + d, at], source, fan_index, i + 1, ratio, inverse,
+                parts, lambda d, at: mid[i + d, at], source, fan_index, i + 1, ratio, inverse,
                 lambda tile, here, value: put(i, tile, here, value),
             )
             return carry
 
         lax.fori_loop(0, planes, plane, 0)
 
+    every = range(PARTS)
+    front, back = range(PARTS // 2), range(PARTS // 2, PARTS)
+    all_planes = (planes + 2, lambda turn: turn)
+    inner = (planes - 2, lambda turn: turn + 2)
+    outer = (4, lambda turn: turn + turn // 2 * (planes - 2))
+
     def step(s, keep, more):
         slot = lax.rem(s, 2)
         other = 1 - slot
-
-        @pl.when(s > 0)
-        def _():
-            wait_edges(cur_copy(slot))
 
         fan_index = fan[k * steps + s]
         wide = cur.at[slot]
@@ -228,12 +257,26 @@
             if keep:
                 states[s, i, tile] = value
 
-        first_sweep(wide, fan_index, 1.0, heat_of)
-        second_sweep(wide, fan_index, 1.0, heat_of, put)
-
-        @pl.when(more)
-        def _():
-            both(cur_copy(other), begin)
+        def arrived(half):
+            @pl.when(s > 0)
+            def _():
+                wait_edges(cur_copy(slot, half))
+
+        def leave(half):
+            @pl.when(more)
+            def _():
+                both(cur_copy(other, half), begin)
+
+        first_sweep(every, inner, wide, fan_index, 1.0, heat_of)
+        arrived(0)
+        first_sweep((0,), outer, wide, fan_index, 1.0, heat_of)
+        arrived(1)
+        first_sweep((1, 2), outer, wide, fan_index, 1.0, heat_of)
+        second_sweep(front, wide, fan_index, 1.0, heat_of, put)
+        leave(0)
+        first_sweep((3,), outer, wide, fan_index, 1.0, heat_of)
+        second_sweep(back, wide, fan_index, 1.0, heat_of, put)
+        leave(1)
 
     start[...] = cur[0]
 
@@ -260,8 +303,8 @@
         corr[i, tile] = value
         states[steps - 1, i, tile] = own_guess[i, tile] + value
 
-    first_sweep(inc, coarse_fan, coarse, None)
-    second_sweep(inc, coarse_fan, coarse, None, put_corr)
+    first_sweep(every, all_planes, inc, coarse_fan, coarse, None)
+    second_sweep(every, inc, coarse_fan, coarse, None, put_corr)
 
     @pl.when(has_after)
     def _():
@@ -285,13 +328,10 @@
     blocks, slabs = lax.axis_size("tm"), lax.axis_size("space")
     planes, ny, nz = initial.shape
     steps, racks = power.shape
-    rack_wide = padded_1(rack_map)
-    heat_wide = padded_1(heat_shape)
-    onehot = (rack_wide[:, :, None] == lax.iota(jnp.int32, racks)[None, None, :]).astype(jnp.float32)
-    cell_power = jnp.einsum(
-        "xyr,kr->kxy", onehot, power.astype(jnp.float32), precision=lax.Precision.HIGHEST
-    )
-    heat = heat_wide[None] * cell_power[:, :, :, None]
+    width = -(-racks // 128) * 128
+    onehot = (rack_map[:, :, None] == lax.iota(jnp.int32, width)[None, None, :]).astype(jnp.float32)
+    levels = jnp.pad(power.astype(jnp.float32), ((0, 0), (0, width - racks)))
+    levels = jnp.broadcast_to(levels[:, :, None], (steps, width, nz))
     tall = ny + 2 * PAD
     vmem = pl.BlockSpec(memory_space=pltpu.VMEM)
     hbm = pl.BlockSpec(memory_space=pl.ANY)
@@ -299,9 +339,12 @@
     return pl.pallas_call(
         functools.partial(kernel, blocks, slabs),
         out_shape=jax.ShapeDtypeStruct((steps, planes, ny, nz), f32),
-        in_specs=[pl.BlockSpec(memory_space=pltpu.SMEM), hbm, hbm, hbm, vmem],
+        in_specs=[pl.BlockSpec(memory_space=pltpu.SMEM), hbm, hbm, hbm, vmem, vmem, vmem],
         out_specs=vmem,
         scratch_shapes=[
+            pltpu.VMEM((steps, planes + 2, ny, nz), f32),
+            pltpu.VMEM((planes + 2, ny, nz), f32),
+            pltpu.VMEM((planes + 2, ny, width), f32),
             pltpu.VMEM((2, planes + 4, tall, nz), f32),
             pltpu.VMEM((planes + 2, tall, nz), f32),
             pltpu.VMEM((planes + 4, tall, nz), f32),
@@ -310,20 +353,24 @@
             pltpu.VMEM((planes, ny, nz), f32),
             pltpu.VMEM((planes, ny, nz), f32),
             pltpu.VMEM((velocity.shape[0], 3, planes + 2, ny, nz), f32),
-            pltpu.SemaphoreType.DMA((2, 2)),
-            pltpu.SemaphoreType.DMA((2, 2)),
-            pltpu.SemaphoreType.DMA((2,)),
-            pltpu.SemaphoreType.DMA((2,)),
-            pltpu.SemaphoreType.DMA((2,)),
-            pltpu.SemaphoreType.DMA((2,)),
-            pltpu.SemaphoreType.DMA((2,)),
-            pltpu.SemaphoreType.DMA((2,)),
-            pltpu.SemaphoreType.DMA((3,)),
+            pltpu.SemaphoreType.DMA((2, 2, 2)),
+            pltpu.SemaphoreType.DMA((2, 2, 2)),
+            pltpu.SemaphoreType.DMA((2,)),
+            pltpu.SemaphoreType.DMA((2,)),
+            pltpu.SemaphoreType.DMA((2,)),
+            pltpu.SemaphoreType.DMA((2,)),
+            pltpu.SemaphoreType.DMA((2,)),
+            pltpu.SemaphoreType.DMA((2,)),
+            pltpu.SemaphoreType.DMA((2,)),
+            pltpu.SemaphoreType.DMA((2,)),
+            pltpu.SemaphoreType.DMA((2,)),
+            pltpu.SemaphoreType.DMA((2,)),
+            pltpu.SemaphoreType.DMA((5,)),
         ],
         compiler_params=pltpu.CompilerParams(
             collective_id=0, has_side_effects=True, vmem_limit_bytes=40 * 1024 * 1024
         ),
-    )(fan_mode, initial, guess, velocity, heat)
+    )(fan_mode, initial, guess, velocity, heat_shape, onehot, levels)
 
 
 def solution(mesh):

time: 213 us -> 196 us (0.920)
  starting transfers between devices: 11.4 us -> 0 us
  Pallas kernels: 191 us -> 186 us
  local copies, waits for them, and re-layouts: 3.79 us -> 7.74 us
    ppermute x4 -> x0, starting transfers between devices: 11.4 us -> none  [the longest x2 7.53 us: padded_1(): before = lax.ppermute(x[length - 1:], 'space', up)]
    unnamed x9 -> x11, local copies, waits for them, and re-layouts: 2.03 us -> 7.41 us
    pallas_call x1, Pallas kernels: 191 us -> 186 us  [local(): pl.pallas_call(functools.partial(kernel, blocks, slabs), out_shape=jax.Sh...]
  transfers between devices with their start and end apart: 4 -> 0, of which waited for: 1 -> 0; matrix products, arithmetic and copies ran while one was open for 1% -> 0% of each run, Pallas kernels for 0% -> 0%
where the time goes in v2:
time: 196 us
  Pallas kernels  186 us (95%)
  local copies, waits for them, and re-layouts  7.74 us (4%)
    pallas_call x1, Pallas kernels, local(): pl.pallas_call(functools.partial(kernel, blocks, slabs), out_shape=jax.Sh...  186 us
    unnamed x11, local copies, waits for them, and re-layouts  7.41 us

profile of v2, /device:TPU:15, one launch (start us, length us, event | category | flops | bytes accessed | tf_op | source)
XLA Modules:
  0.0 195.8 jit_solution(7641905871172497759)
XLA Ops:
  0.0 0.7 convert_element_type.9
  0.7 0.8 fusion.onehot_own
  1.5 0.3 broadcast_in_dim.2.levels
  1.9 0.0 copy-start
  1.9 1.9 copy-done
  3.8 0.0 copy-start.1
  3.8 0.9 copy-done.1
  4.7 0.0 copy-start.2
  4.7 0.9 copy-done.2
  5.7 0.0 copy-start.3
  5.7 0.9 copy-done.3
  6.6 0.0 copy-start.4
  6.6 0.7 copy-done.4
  7.3 186.5 %shard_map.73 = f32[16,4,128,128]{3,2,1,0:T(8,128)S(1)} custom-call(s32[64]{0:T(128)S(1)} %copy-done.4, f32[4,128,128]{2,1,0:T(8,128)S(1)} %copy-done.1, f32[1,4,128,128]{3,2,1,0:T(8,128)S(1)} %copy-done.2, f32[4,3,4,128,128]{4,3,2,1,0:T(8,128)S(1)} %copy-done, f32[4,128,128]{2,1,0:T(8,128)S(1)} %copy-done.3, f32[4,128,128]{2,1,0:T(8,128)S(1)} %fusion.onehot_own, ...), custom_call_target="tpu_custom_call" | custom-call | tf_op jit(solution)/shard_map/pallas_call | solution.py:339
  193.7 2.0 %copy.9 = f32[16,4,128,128]{3,2,1,0:T(8,128)} copy(f32[16,4,128,128]{3,2,1,0:T(8,128)S(1)} %shard_map.73) | data formatting | bytes 8388608
  (1 shorter events, 0.0 us)
Async XLA Ops:
  1.9 1.9 copy-start
  3.8 0.9 copy-start.1
  4.7 0.9 copy-start.2
  5.7 0.9 copy-start.3
  6.6 0.7 copy-start.4
